TPU v7x, 32 devices: a whole 2x2x4 slice. The times are simulated.
32 devices in a mesh: cuts: 4 (over y, x), dev: 8 (over z, core).
Axes of the slice: x: 2, y: 2, z: 4, core: 2. Of those that a mesh axis runs over, the one named last changes fastest.
Arguments:
- kv_cache: bfloat16 [256, 128, 2048], P(('cuts', 'dev')), may hold values from -6 to 6
- queries: bfloat16 [4, 8, 768, 128], P('cuts', 'dev'), may hold values from -6 to 6
- gates: bfloat16 [4, 1, 768, 1024], P('cuts', None, 'dev'), may hold values from -6 to 6
- tokens: bfloat16 [4, 1, 768, 1024], P('cuts', None, 'dev'), may hold values from -6 to 6
- w_out: bfloat16 [1024, 1024], P('dev'), may hold values from -0.1875 to 0.1875
- norm_gain: float32 [1024], replicated, may hold values from 0.1 to 1.9
- hist_blocks: int32 [4, 4], replicated, may hold values from 1 to 32, as said below
- ranker_list: int32 [4, 4], replicated, may hold values from 0 to 3, as said below
- owner_ids: int32 [4, 4, 32], replicated, may hold values from -1 to 31, as said below
- slot_ids: int32 [4, 4, 32], replicated, may hold values from -1 to 7, as said below
- block_mask: int32 [4, 4, 6, 32], replicated, may hold values 0 or 1
Outputs:
- mixed: bfloat16 [4, 1, 768, 1024], P('cuts', None, 'dev')
Inputs may be any that keep to these rules, and one draw needn't show every extreme that they name: `hist_blocks`: the entries of one slice sum to 64, and one request of each slice has exactly 32 blocks. `ranker_list`: each slice's row is a permutation of its 4 requests. `owner_ids`: an entry is the cut index times 8 plus the dev index of the device that holds the block, and -1 exactly where b >= hist_blocks. Every device holds exactly 2 blocks of each slice's requests. The blocks of the 4 requests of one ranker group lie on devices of one dev index (over all cuts) at most 8 times, and some group reaches 8. `slot_ids`: -1 exactly where owner_ids is -1; the blocks of all slices use every cache row of every device exactly once.
All inputs are finite; a program needn't handle non-finite values.
Results may differ from a plain program's by a relative error of at most 0.0046.
Values may be sent and summed in bfloat16 or wider, within the bound.
A program may use at most 128 MiB of HBM per device.

v0:
```python
import jax
import jax.numpy as jnp
from jax import lax
from jax.sharding import PartitionSpec as P

H = 8
DH = 128
HB = 32
RQ = 4
TILE = 32


EPS = 1e-05


def ranked(selected, count):
    sequence = jnp.cumsum(selected.astype(jnp.int32), axis=-1) - 1
    picks = jnp.arange(count, dtype=jnp.int32)
    return selected[..., None, :] & (sequence[..., None, :] == picks[:, None])


def local(
    kv_cache,
    queries,
    gates,
    tokens,
    w_out,
    norm_gain,
    hist_blocks,
    ranker_list,
    owner_ids,
    slot_ids,
    block_mask,
):
    cut_count = lax.axis_size("cuts")
    dev_count = lax.axis_size("dev")
    this_cut = lax.axis_index("cuts")
    this_dev = lax.axis_index("dev")
    groups = dev_count // H
    group_index = this_dev % groups
    pool_size, block_items, width = kv_cache.shape
    slab_width = width // H
    head_size = slab_width // 2
    owned = pool_size // cut_count
    per_group = RQ * HB
    live_cut = owned * cut_count * dev_count
    capacity = (min(per_group, live_cut) + dev_count - 1) // dev_count
    request_count = ranker_list.shape[1]
    keys_cut = request_count * HB
    cut_rows = jnp.arange(cut_count)[:, None]
    owners_ranked = owner_ids[cut_rows, ranker_list].reshape(cut_count, keys_cut)
    slots_ranked = slot_ids[cut_rows, ranker_list].reshape(cut_count, keys_cut)
    owner_self = this_cut * dev_count + this_dev
    chosen = ranked(owners_ranked == owner_self, owned)
    send_rows = jnp.sum(jnp.where(chosen, slots_ranked[:, None, :], 0), axis=-1)
    packed = kv_cache[send_rows.reshape(-1)].reshape(cut_count, owned, block_items, width)
    arrived = lax.all_to_all(packed, "cuts", split_axis=0, concat_axis=0, tiled=True)
    owner_table = lax.dynamic_index_in_dim(owners_ranked, this_cut, 0, keepdims=False)
    sources = jnp.arange(cut_count, dtype=jnp.int32) * dev_count + this_dev
    relay_pick = ranked(owner_table[None, :] == sources[:, None], owned)
    key_index = jnp.arange(keys_cut, dtype=jnp.int32)
    key_of = jnp.sum(jnp.where(relay_pick, key_index, 0), axis=-1).reshape(pool_size)
    group_of = key_of // per_group
    sequence = jnp.arange(pool_size)
    earlier = (group_of[None, :] == group_of[:, None]) & (sequence[None, :] < sequence[:, None])
    target = group_of * capacity + jnp.sum(earlier, axis=1)
    heads_first = arrived.reshape(pool_size, block_items, H, slab_width).transpose(2, 0, 1, 3)
    outgoing = jnp.zeros((H, groups * capacity, block_items, slab_width), arrived.dtype)
    outgoing = (
        outgoing.at[:, target]
        .set(heads_first)
        .reshape(dev_count, capacity, block_items, slab_width)
    )
    received = lax.all_to_all(outgoing, "dev", split_axis=0, concat_axis=0, tiled=True)
    flat_blocks = received.reshape(dev_count * capacity, block_items, slab_width)
    cut_list = lax.dynamic_index_in_dim(ranker_list, this_cut, 0, keepdims=False)
    requests = lax.dynamic_slice_in_dim(cut_list, group_index * RQ, RQ)
    lengths = lax.dynamic_index_in_dim(hist_blocks, this_cut, 0, keepdims=False)[requests]
    group_mask = lax.dynamic_index_in_dim(block_mask, this_cut, 0, keepdims=False)[requests]
    live_blocks = jnp.arange(HB, dtype=jnp.int32)[None, :] < lengths[:, None]
    is_live = live_blocks.reshape(per_group)
    group_owners = lax.dynamic_slice_in_dim(owner_table, group_index * per_group, per_group)
    src_dev = group_owners % dev_count
    src_cut = group_owners // dev_count
    position = jnp.arange(per_group)
    before = (
        is_live[None, :]
        & (src_dev[None, :] == src_dev[:, None])
        & (
            (src_cut[None, :] < src_cut[:, None])
            | (src_cut[None, :] == src_cut[:, None]) & (position[None, :] < position[:, None])
        )
    )
    slot_of = jnp.where(is_live, src_dev * capacity + jnp.sum(before, axis=1), 0).reshape(RQ, HB)
    tile_mask = (group_mask * live_blocks[:, None, :].astype(jnp.int32)).astype(jnp.float32)
    query_all = queries.reshape(RQ, -1, head_size)

    def attend(query, slot_rows, tiles):
        blocks = flat_blocks[slot_rows]
        key_rows = blocks[:, :, :head_size].reshape(-1, head_size)
        value_rows = blocks[:, :, head_size:].reshape(-1, head_size)
        scores = jnp.einsum(
            "ce,ke->ck", query, key_rows, preferred_element_type=jnp.float32
        ) * DH ** (-0.5)
        allowed = jnp.repeat(tiles, TILE, axis=0)
        rows_here = query.shape[0]
        weights = jax.nn.silu(scores).reshape(rows_here, HB, block_items) * allowed[:, :, None]
        weights = weights.reshape(rows_here, -1).astype(jnp.bfloat16)
        return jnp.dot(weights, value_rows, preferred_element_type=jnp.float32).astype(jnp.bfloat16)

    attended = lax.map(
        lambda parts: attend(parts[0], parts[1], parts[2]), (query_all, slot_of, tile_mask)
    )
    rows_each = attended.shape[0] * attended.shape[1] // dev_count
    back = lax.all_to_all(
        attended.reshape(dev_count, rows_each, head_size),
        "dev",
        split_axis=0,
        concat_axis=0,
        tiled=True,
    )
    gathered = back.reshape(H, groups, rows_each, head_size).transpose(1, 2, 0, 3)
    gathered = gathered.reshape(groups * rows_each, H * head_size).astype(jnp.float32)
    row_mean = jnp.mean(gathered, axis=-1, keepdims=True)
    centred = gathered - row_mean
    variance = jnp.mean(centred * centred, axis=-1, keepdims=True)
    normed = centred * lax.rsqrt(variance + EPS) * norm_gain
    gate_rows = gates.reshape(-1, H * head_size).astype(jnp.float32)
    gated = (normed * jax.nn.silu(gate_rows)).astype(jnp.bfloat16)
    projected = jnp.dot(
        gated, lax.all_gather(w_out, "dev", axis=0, tiled=True), preferred_element_type=jnp.float32
    )
    return (tokens.astype(jnp.float32) + projected.reshape(tokens.shape)).astype(jnp.bfloat16)


def solution(mesh):
    return jax.shard_map(
        local,
        mesh=mesh,
        in_specs=(
            P(("cuts", "dev"), None, None),
            P("cuts", "dev", None, None),
            P("cuts", None, "dev", None),
            P("cuts", None, "dev", None),
            P("dev", None),
            P(),
            P(),
            P(),
            P(),
            P(),
            P(),
        ),
        out_specs=P("cuts", None, "dev", None),
        check_vma=False,
    )
```

profile of v0, /device:TPU:0, one launch (start us, length us, event | category | flops | bytes accessed | tf_op | source)
XLA Modules:
  0.0 274.2 jit_solution(3266043263519407009)
XLA Ops:
  6.5 0.7 fusion.46
  7.3 1.3 gather_fusion.2
  9.0 1.3 gather_fusion.3
  10.8 4.9 %gather_fusion.4 = bf16[8,128,2048]{2,1,0:T(8,128)(2,1)} fusion(bf16[8,128,2048]{2,1,0:T(8,128)(2,1)} %param.13, s32[1024]{0:T(1024)S(1)} %pad_clamp_fusion.1), kind=kCustom, calls=%fused_computation.4 | custom fusion | bytes 8388640 | tf_op jit(solution)/shard_map/gather | solution.py:56
  15.7 6.4 %copy.23 = bf16[8,128,2048]{1,2,0:T(8,128)(2,1)} copy(bf16[8,128,2048]{2,1,0:T(8,128)(2,1)} %gather_fusion.4) | data formatting | bytes 8388608 | tf_op jit(solution)/shard_map/gather | solution.py:56
  22.2 5.2 %all-to-all-start = ((bf16[4,2,128,2048]{2,3,1,0:T(8,128)(2,1)}), bf16[4,2,128,2048]{2,3,1,0:T(8,128)(2,1)}, u32[]{:S(2)}, u32[]{:S(2)}) async-start(bf16[4,2,128,2048]{2,3,1,0:T(8,128)(2,1)} %bitcast.145), calls=%async_computation | async-start | bytes 8388608 | tf_op jit(solution)/shard_map/all_to_all | solution.py:57
  29.4 46.5 %all-to-all-done = bf16[4,2,128,2048]{2,3,1,0:T(8,128)(2,1)} async-done(((bf16[4,2,128,2048]{2,3,1,0:T(8,128)(2,1)}), bf16[4,2,128,2048]{2,3,1,0:T(8,128)(2,1)}, u32[]{:S(2)}, u32[]{:S(2)}) %all-to-all-start) | async-done | bytes 4194336 | tf_op jit(solution)/shard_map/all_to_all | solution.py:57
  75.9 6.5 %copy.24 = bf16[8,8,128,256]{3,2,1,0:T(8,128)(2,1)} copy(bf16[8,8,128,256]{2,3,1,0:T(8,128)(2,1)} %bitcast.21) | data formatting | bytes 8388608 | tf_op jit(solution)/shard_map/transpose | solution.py:67
  82.4 2.5 broadcast_in_dim.37
  84.9 10.9 %scatter_fusion = bf16[8,8,128,256]{3,2,1,0:T(8,128)(2,1)} fusion(bf16[8,8,128,256]{3,2,1,0:T(8,128)(2,1)} %broadcast_in_dim.37, s32[8]{0:T(128)S(1)} %fusion.50, bf16[8,8,128,256]{3,2,1,0:T(8,128)(2,1)} %copy.24), kind=kCustom, calls=%fused_computation.6 | custom fusion | bytes 12582944 | tf_op jit(solution)/shard_map/scatter | solution.py:71
  95.8 5.1 %all-to-all-start.1 = ((bf16[8,8,128,256]{3,2,1,0:T(8,128)(2,1)}), bf16[8,8,128,256]{3,2,1,0:T(8,128)(2,1)}, u32[]{:S(2)}, u32[]{:S(2)}) async-start(bf16[8,8,128,256]{3,2,1,0:T(8,128)(2,1)} %scatter_fusion), calls=%async_computation.1 | async-start | bytes 8388608 | tf_op jit(solution)/shard_map/all_to_all | solution.py:74
  101.6 0.7 fusion.52
  104.8 107.0 %all-to-all-done.1 = bf16[8,8,128,256]{3,2,1,0:T(8,128)(2,1)} async-done(((bf16[8,8,128,256]{3,2,1,0:T(8,128)(2,1)}), bf16[8,8,128,256]{3,2,1,0:T(8,128)(2,1)}, u32[]{:S(2)}, u32[]{:S(2)}) %all-to-all-start.1) | async-done | bytes 4194336 | tf_op jit(solution)/shard_map/all_to_all | solution.py:74
  211.8 41.2 %while.10 = (s32[]{:T(128)}, bf16[4,192,128]{2,1,0:T(8,128)(2,1)S(1)}, bf16[4,192,128]{2,1,0:T(8,128)(2,1)}, s32[4,32]{1,0:T(4,128)S(1)}, bf16[64,128,256]{2,1,0...) while((s32[]{:T(128)}, bf16[4,192,128]{2,1,0:T(8,128)(2,1)S(1)}, bf16[4,192,128]{2,1,0:T(8,128)(2,1)}, ...), condition=%wide.region_8.9_spmd, body=%wide.region_7.8_spmd.sunk | while | flops 408183904 | bytes 16932692 | solution.py:111
  211.9 2.9 %gather_fusion = bf16[32,128,256]{2,1,0:T(8,128)(2,1)S(1)} fusion(bf16[64,128,256]{2,1,0:T(8,128)(2,1)} %get-tuple-element.123, s32[1024]{0:T(1024)S(1)} %pad_clamp_fusion.4), kind=kCustom, calls=%fused_computation.clone.1 | custom fusion | bytes 4194432 | tf_op jit(solution)/shard_map/while/body/eval_jaxpr/gather | solution.py:99
  214.7 1.9 fusion.73
  216.7 0.9 mul.178
  217.6 4.6 %fusion.74 = bf16[4,192,128]{2,1,0:T(8,128)(2,1)S(1)} fusion(bf16[4,192,128]{2,1,0:T(8,128)(2,1)S(1)} %get-tuple-element.113, s32[]{:T(128)} %get-tuple-element.112, bf16[4096,128]{1,0:T(8,128)(2,1)} %bitcast.144, f32[24,8,32,128]{3,2,1,0:T(8,128)S(1)} %bitcast.142, bf16[4096,128]{1,0:T(8,128)(2,1)} %bitcast.143, ...), kind=kOutput, calls=%fused_computation.13.clone.1 | convolution fusion | flops 408182784 | bytes 5342208 | tf_op jit(solution)/shard_map/while/body/eval_jaxpr/dot_general | solution.py:109
  222.2 2.9 %gather_fusion = bf16[32,128,256]{2,1,0:T(8,128)(2,1)S(1)} fusion(bf16[64,128,256]{2,1,0:T(8,128)(2,1)} %get-tuple-element.123, s32[1024]{0:T(1024)S(1)} %pad_clamp_fusion.4), kind=kCustom, calls=%fused_computation.clone.1 | custom fusion | bytes 4194432 | tf_op jit(solution)/shard_map/while/body/eval_jaxpr/gather | solution.py:99
  225.1 1.9 fusion.73
  227.0 0.9 mul.178
  227.9 4.6 %fusion.74 = bf16[4,192,128]{2,1,0:T(8,128)(2,1)S(1)} fusion(bf16[4,192,128]{2,1,0:T(8,128)(2,1)S(1)} %get-tuple-element.113, s32[]{:T(128)} %get-tuple-element.112, bf16[4096,128]{1,0:T(8,128)(2,1)} %bitcast.144, f32[24,8,32,128]{3,2,1,0:T(8,128)S(1)} %bitcast.142, bf16[4096,128]{1,0:T(8,128)(2,1)} %bitcast.143, ...), kind=kOutput, calls=%fused_computation.13.clone.1 | convolution fusion | flops 408182784 | bytes 5342208 | tf_op jit(solution)/shard_map/while/body/eval_jaxpr/dot_general | solution.py:109
  232.5 2.9 %gather_fusion = bf16[32,128,256]{2,1,0:T(8,128)(2,1)S(1)} fusion(bf16[64,128,256]{2,1,0:T(8,128)(2,1)} %get-tuple-element.123, s32[1024]{0:T(1024)S(1)} %pad_clamp_fusion.4), kind=kCustom, calls=%fused_computation.clone.1 | custom fusion | bytes 4194432 | tf_op jit(solution)/shard_map/while/body/eval_jaxpr/gather | solution.py:99
  235.4 1.9 fusion.73
  237.3 0.9 mul.178
  238.2 4.6 %fusion.74 = bf16[4,192,128]{2,1,0:T(8,128)(2,1)S(1)} fusion(bf16[4,192,128]{2,1,0:T(8,128)(2,1)S(1)} %get-tuple-element.113, s32[]{:T(128)} %get-tuple-element.112, bf16[4096,128]{1,0:T(8,128)(2,1)} %bitcast.144, f32[24,8,32,128]{3,2,1,0:T(8,128)S(1)} %bitcast.142, bf16[4096,128]{1,0:T(8,128)(2,1)} %bitcast.143, ...), kind=kOutput, calls=%fused_computation.13.clone.1 | convolution fusion | flops 408182784 | bytes 5342208 | tf_op jit(solution)/shard_map/while/body/eval_jaxpr/dot_general | solution.py:109
  242.8 2.9 %gather_fusion = bf16[32,128,256]{2,1,0:T(8,128)(2,1)S(1)} fusion(bf16[64,128,256]{2,1,0:T(8,128)(2,1)} %get-tuple-element.123, s32[1024]{0:T(1024)S(1)} %pad_clamp_fusion.4), kind=kCustom, calls=%fused_computation.clone.1 | custom fusion | bytes 4194432 | tf_op jit(solution)/shard_map/while/body/eval_jaxpr/gather | solution.py:99
  245.7 1.9 fusion.73
  247.6 0.9 mul.178
  248.5 4.6 %fusion.74 = bf16[4,192,128]{2,1,0:T(8,128)(2,1)S(1)} fusion(bf16[4,192,128]{2,1,0:T(8,128)(2,1)S(1)} %get-tuple-element.113, s32[]{:T(128)} %get-tuple-element.112, bf16[4096,128]{1,0:T(8,128)(2,1)} %bitcast.144, f32[24,8,32,128]{3,2,1,0:T(8,128)S(1)} %bitcast.142, bf16[4096,128]{1,0:T(8,128)(2,1)} %bitcast.143, ...), kind=kOutput, calls=%fused_computation.13.clone.1 | convolution fusion | flops 408182784 | bytes 5342208 | tf_op jit(solution)/shard_map/while/body/eval_jaxpr/dot_general | solution.py:109
  253.1 10.7 %all_to_all.15 = bf16[8,96,128]{2,1,0:T(8,128)(2,1)S(1)} all-to-all(bf16[8,96,128]{2,1,0:T(8,128)(2,1)S(1)} %bitcast.148), channel_id=1, replica_groups=mesh['cuts'=4,'dev'=8] {'dev'}, dimensions={0} | all-to-all | bytes 393216 | tf_op jit(solution)/shard_map/all_to_all | solution.py:115
  264.5 2.9 %fusion.16 = bf16[1,1,96,1024]{3,2,1,0:T(8,128)(2,1)} fusion(bf16[1024,1024]{1,0:T(8,128)(2,1)} %all-gather.2.cloned.1.call-done, bf16[1,1,96,1024]{3,2,1,0:T(8,128)(2,1)} %param.16, f32[12,8,8,128]{3,2,1,0:T(8,128)S(1)} %bitcast.147, bf16[1,1,96,1024]{3,2,1,0:T(8,128)(2,1)} %param.15, f32[1024]{0:T(1024)S(1)} %copy-done.1, f32[96]{0:T(128)S(1)} %add_rsqrt_fusion, ...), kind=kOutput, calls=%fused_computation.27 | convolution fusion | flops 202604544 | bytes 3085056 | tf_op jit(solution)/shard_map/dot_general | solution.py:130
  (69 shorter events, 6.9 us)
Async XLA Ops:
  6.5 97.7 %copy-start = (s32[4,4,6,32]{3,1,2,0:T(4,128)S(1)}, s32[4,4,6,32]{3,1,2,0:T(4,128)}, u32[]{:S(2)}) copy-start(s32[4,4,6,32]{3,1,2,0:T(4,128)} %param.23) | copy-start | bytes 36868
  22.2 53.8 %all-to-all-start = ((bf16[4,2,128,2048]{2,3,1,0:T(8,128)(2,1)}), bf16[4,2,128,2048]{2,3,1,0:T(8,128)(2,1)}, u32[]{:S(2)}, u32[]{:S(2)}) async-start(bf16[4,2,128,2048]{2,3,1,0:T(8,128)(2,1)} %bitcast.145), calls=%async_computation | async-start | bytes 8388608 | tf_op jit(solution)/shard_map/all_to_all | solution.py:57
  95.8 116.0 %all-to-all-start.1 = ((bf16[8,8,128,256]{3,2,1,0:T(8,128)(2,1)}), bf16[8,8,128,256]{3,2,1,0:T(8,128)(2,1)}, u32[]{:S(2)}, u32[]{:S(2)}) async-start(bf16[8,8,128,256]{3,2,1,0:T(8,128)(2,1)} %scatter_fusion), calls=%async_computation.1 | async-start | bytes 8388608 | tf_op jit(solution)/shard_map/all_to_all | solution.py:74
  100.9 163.6 %all-gather.2.cloned.1.call-start = ((), (), s32[]{:S(2)}) async-start(), calls=%async_computation.3 | async-start | bytes 2359296 | tf_op jit(solution)/shard_map/all_gather | solution.py:131
  211.8 52.6 %copy-start.1 = (f32[1024]{0:T(1024)S(1)}, f32[1024]{0:T(1024)}, u32[]{:S(2)}) copy-start(f32[1024]{0:T(1024)} %param.18) | copy-start | bytes 12292
Sparse Core Ops, SparseCore 0:
  103.3 49.6 all-gather.1
where the time goes:
time: 275 us; the launch traced here: 274 us
  waiting for transfers between devices  154 us (56%)
  local copies, waits for them, and re-layouts  60.8 us (22%)
  matrix products  21.1 us (8%)
  between operations  13.5 us (5%)
  blocking collectives  10.7 us (4%)
  starting transfers between devices  10.3 us (4%)
  other arithmetic  3.4 us (1%)
    all_to_all x1, waiting for transfers between devices, local(): lax.all_to_all(outgoing, 'dev', split_axis=0, concat_axis=0, tiled=True)  107 us
    all_to_all x1, waiting for transfers between devices, local(): lax.all_to_all(packed, 'cuts', split_axis=0, concat_axis=0, tiled=True)  46.5 us
    dot_general x4, matrix products, attend(): jnp.dot(weights, value_rows, preferred_element_type=jnp.float32)  18.2 us
    gather x4, local copies, waits for them, and re-layouts, attend(): blocks = flat_blocks[slot_rows]  11.5 us
    gather x2, local copies, waits for them, and re-layouts, local(): kv_cache[send_rows.reshape(-1)]  11.4 us
    scatter x1, local copies, waits for them, and re-layouts, local(): outgoing = outgoing.at[:, target].set(heads_first).reshape(dev_count, cap...  10.9 us
    all_to_all x1, blocking collectives, local(): lax.all_to_all(attended.reshape(dev_count, rows_each, head_size), 'dev',...  10.7 us
    slice x4, local copies, waits for them, and re-layouts, attend(): key_rows = blocks[:, :, :head_size].reshape(-1, head_size)  7.8 us
  transfers between devices with their start and end apart: 3, of which 2 were waited for; matrix products, arithmetic and copies ran while one was open for 17% of the time, Pallas kernels for 0%

commit v1 on v0

--- a/solution.py
+++ b/solution.py
@@ -1,6 +1,10 @@
+import functools
+
 import jax
 import jax.numpy as jnp
 from jax import lax
+from jax.experimental import pallas as pl
+from jax.experimental.pallas import tpu as pltpu
 from jax.sharding import PartitionSpec as P
 
 H = 8
@@ -19,7 +23,7 @@
     return selected[..., None, :] & (sequence[..., None, :] == picks[:, None])
 
 
-def local(
+def local_general(
     kv_cache,
     queries,
     gates,
@@ -133,7 +137,375 @@
     return (tokens.astype(jnp.float32) + projected.reshape(tokens.shape)).astype(jnp.bfloat16)
 
 
+CUTS = 4
+DEVS = 8
+STAGES = 4
+MESH = pl.DeviceIdType.MESH
+
+
+def rem(a, b):
+    return lax.rem(a, jnp.int32(b))
+
+
+def div(a, b):
+    return lax.div(a, jnp.int32(b))
+
+
+def fused_kernel(
+    rows_ref,
+    mask_ref,
+    q_ref,
+    gates_ref,
+    tokens_ref,
+    w_ref,
+    gain_ref,
+    kv_ref,
+    out_ref,
+    kv0,
+    kv1,
+    kv2,
+    kv3,
+    pk,
+    rx,
+    qbuf,
+    acc,
+    ab,
+    parts,
+    wbuf,
+    load_sem,
+    kv_send,
+    kv_recv,
+    q_send,
+    q_recv,
+    p_send,
+    p_recv,
+    w_send,
+    w_recv,
+):
+    loaded = (kv0, kv1, kv2, kv3)
+    cut = lax.axis_index("cuts")
+    dev = lax.axis_index("dev")
+    x, y = rem(cut, 2), div(cut, 2)
+    z, core = div(dev, 2), rem(dev, 2)
+
+    def cut_at(off):
+        return rem(y + div(off, 2), 2) * 2 + rem(x + rem(off, 2), 2)
+
+    def core_at(off):
+        return rem(core + off, 2)
+
+    def load(s, oh):
+        head = rem(z + s, 4) * 2 + core_at(oh)
+        columns = pl.ds(pl.multiple_of(head * 256, 256), 256)
+        return pltpu.make_async_copy(
+            kv_ref.at[:, :, columns], loaded[s].at[oh], load_sem.at[s, oh]
+        )
+
+    for s in range(STAGES):
+        for oh in range(2):
+            load(s, oh).start()
+
+    barrier = pltpu.get_barrier_semaphore()
+    for o in range(2, 8):
+        pl.semaphore_signal(
+            barrier,
+            inc=1,
+            device_id=(cut_at(o // 2), z * 2 + core_at(o % 2)),
+            device_id_type=MESH,
+        )
+    for o in range(1, 8):
+        pl.semaphore_signal(
+            barrier,
+            inc=1,
+            device_id=(cut, rem(z + o // 2, 4) * 2 + core_at(o % 2)),
+            device_id_type=MESH,
+        )
+    pl.semaphore_wait(barrier, 13)
+
+    def kv_copy(s, o):
+        return pltpu.make_async_remote_copy(
+            src_ref=pk.at[s, o],
+            dst_ref=rx.at[s, o],
+            send_sem=kv_send.at[s, o],
+            recv_sem=kv_recv.at[s, o],
+            device_id=(cut_at(div(o, 2)), z * 2 + core_at(rem(o, 2))),
+            device_id_type=MESH,
+        )
+
+    def q_copy(o):
+        return pltpu.make_async_remote_copy(
+            src_ref=q_ref,
+            dst_ref=qbuf.at[4 - o],
+            send_sem=q_send.at[4 - o],
+            recv_sem=q_recv.at[4 - o],
+            device_id=(cut, rem(z + o, 4) * 2 + core),
+            device_id_type=MESH,
+        )
+
+    def p_copy(s, o):
+        where = rem(z + div(o, 2), 4) * 2 + core_at(rem(o, 2))
+        return pltpu.make_async_remote_copy(
+            src_ref=ab.at[s, where],
+            dst_ref=parts.at[s, o],
+            send_sem=p_send.at[s, o],
+            recv_sem=p_recv.at[s, o],
+            device_id=(cut, where),
+            device_id_type=MESH,
+        )
+
+    def w_copy(o):
+        if o % 2:
+            source = w_ref if o == 1 else wbuf.at[o - 1]
+            where = z * 2 + core_at(1)
+        else:
+            source = w_ref
+            where = rem(z + o // 2, 4) * 2 + core
+        return pltpu.make_async_remote_copy(
+            src_ref=source,
+            dst_ref=wbuf.at[o],
+            send_sem=w_send.at[o],
+            recv_sem=w_recv.at[o],
+            device_id=(cut, where),
+            device_id_type=MESH,
+        )
+
+    def pack(s):
+        for oh in range(2):
+            load(s, oh).wait()
+
+        def one(i, carry):
+            oc = 3 - i
+            for j in range(2):
+                slot = rows_ref[cut_at(oc), j]
+                for oh in range(2):
+                    pk[s, oc * 2 + oh, j] = loaded[s][oh, slot]
+            for oh in range(2):
+
+                @pl.when(oc * 2 + oh > 0)
+                def _():
+                    kv_copy(s, oc * 2 + oh).start()
+
+            return carry
+
+        lax.fori_loop(jnp.int32(0), jnp.int32(4), one, 0)
+        rx[s, 0] = pk[s, 0]
+
+    pack(0)
+    for o in (3, 2, 1):
+        q_copy(o).start()
+    pack(1)
+    for o in (6, 4, 2, 1):
+        w_copy(o).start()
+    qbuf[0] = q_ref[...]
+
+    def stage(s, carry):
+        @pl.when(s > 0)
+        def _():
+            q_copy(4 - s).wait_recv()
+
+        acc[...] = jnp.zeros_like(acc)
+
+        def block(o, inner):
+            @pl.when(o > 0)
+            def _():
+                kv_copy(s, o).wait_recv()
+
+            keys = rx[s, o, :, :, 0:128].reshape(256, 128)
+            values = rx[s, o, :, :, 128:256].reshape(256, 128)
+            for k in range(RQ):
+                rows = pl.ds(k * 192, 192)
+                scores = lax.dot_general(
+                    qbuf[s, rows, :],
+                    keys,
+                    (((1,), (1,)), ((), ())),
+                    preferred_element_type=jnp.float32,
+                )
+                half = scores.reshape(6, TILE, 256) * mask_ref[o, k][:6, None, :]
+                weights = (half + half * jnp.tanh(half)).reshape(192, 256)
+                acc[rows, :] += jnp.dot(
+                    weights.astype(jnp.bfloat16), values, preferred_element_type=jnp.float32
+                )
+            return inner
+
+        lax.fori_loop(jnp.int32(0), jnp.int32(8), block, 0)
+        ab[s] = acc[...].reshape(8, 96, 128).astype(jnp.bfloat16)
+
+        def send(o, inner):
+            p_copy(s, o).start()
+            return inner
+
+        lax.fori_loop(jnp.int32(1), jnp.int32(8), send, 0)
+        parts[s, 0] = ab[s, z * 2 + core]
+
+        @pl.when(s == 0)
+        def _():
+            pack(2)
+
+        @pl.when(s == 1)
+        def _():
+            pack(3)
+
+        @pl.when(s == 2)
+        def _():
+            for o in (2, 4, 6):
+                w_copy(o).wait_recv()
+                w_copy(o + 1).start()
+
+        return carry
+
+    lax.fori_loop(jnp.int32(0), jnp.int32(STAGES), stage, 0)
+
+    gate_list, total_list = [], []
+    for pr in range(4):
+        for oh in range(2):
+            head = rem(z + pr, 4) * 2 + core_at(oh)
+            columns = pl.ds(pl.multiple_of(head * 128, 128), 128)
+            gate = gates_ref[:, columns].astype(jnp.float32)
+            gate_list.append(gate / (1.0 + jnp.exp(-gate)) * gain_ref[:, columns])
+    for o in (1, 3, 5, 7):
+        w_copy(o).wait_recv()
+    for s in range(STAGES):
+        for o in range(1, 8):
+            p_copy(jnp.int32(s), jnp.int32(o)).wait_recv()
+    for pr in range(4):
+        for oh in range(2):
+            total = parts[pr, oh].astype(jnp.float32)
+            for ok in range(1, 4):
+                total += parts[(pr + ok) % 4, ok * 2 + oh].astype(jnp.float32)
+            total_list.append(total)
+    features = float(H * DH)
+    mean = jnp.sum(sum(total_list), axis=-1, keepdims=True) / features
+    centred = [total - mean for total in total_list]
+    squares = sum(part * part for part in centred)
+    variance = jnp.sum(squares, axis=-1, keepdims=True) / features
+    scale = lax.rsqrt(variance + EPS)
+    projected = tokens_ref[...].astype(jnp.float32)
+    for pr in range(4):
+        ow = (4 - pr) % 4
+        for oh in range(2):
+            r = pr * 2 + oh
+            gated = (centred[r] * scale * gate_list[r]).astype(jnp.bfloat16)
+            weight = w_ref[...] if ow * 2 + oh == 0 else wbuf[ow * 2 + oh]
+            projected += jnp.dot(gated, weight, preferred_element_type=jnp.float32)
+    out_ref[...] = projected.astype(out_ref.dtype)
+
+    for o in (1, 2, 3):
+        q_copy(o).wait_send()
+    for o in range(1, 8):
+        w_copy(o).wait_send()
+
+    def drain(i, carry):
+        s, o = div(i, 7), rem(i, 7) + 1
+        kv_copy(s, o).wait_send()
+        p_copy(s, o).wait_send()
+        return carry
+
+    lax.fori_loop(jnp.int32(0), jnp.int32(28), drain, 0)
+
+
+def local_fused(
+    kv_cache,
+    queries,
+    gates,
+    tokens,
+    w_out,
+    norm_gain,
+    hist_blocks,
+    ranker_list,
+    owner_ids,
+    slot_ids,
+    block_mask,
+):
+    cut = lax.axis_index("cuts")
+    dev = lax.axis_index("dev")
+    me = cut * DEVS + dev
+    position = jnp.arange(RQ * HB, dtype=jnp.int32)
+    coded = position * DEVS + slot_ids.reshape(CUTS, RQ * HB)
+    mine = owner_ids.reshape(CUTS, RQ * HB) == me
+    first = jnp.min(jnp.where(mine, coded, 1 << 20), axis=-1)
+    last = jnp.max(jnp.where(mine, coded, 0), axis=-1)
+    send_rows = jnp.stack([first, last], axis=-1) % DEVS
+
+    offset = jnp.arange(8, dtype=jnp.int32)
+    sources = (cut ^ (offset // 2)) * DEVS + (dev ^ (offset % 2))
+    owners = lax.dynamic_index_in_dim(owner_ids, cut, 0, keepdims=False).reshape(-1)
+    theirs = owners[None, :] == sources[:, None]
+    lowest = jnp.min(jnp.where(theirs, position, 1 << 20), axis=-1)
+    highest = jnp.max(jnp.where(theirs, position, -1), axis=-1)
+    places = jnp.stack([lowest, highest], axis=-1)
+    live = jnp.arange(HB, dtype=jnp.int32) < lax.dynamic_index_in_dim(
+        hist_blocks, cut, 0, keepdims=False
+    )[:, None]
+    visible = lax.dynamic_index_in_dim(block_mask, cut, 0, keepdims=False) * live[:, None, :]
+    ranks = lax.dynamic_index_in_dim(ranker_list, cut, 0, keepdims=False)
+    is_ranked = ranks[:, None] == jnp.arange(RQ, dtype=jnp.int32)
+    table = jnp.where(is_ranked[:, None, :, None], visible.transpose(1, 0, 2)[None], 0)
+    table = table.reshape(RQ, -1, RQ * HB).astype(jnp.bfloat16)
+    table = jnp.pad(table, ((0, 0), (0, 8 - table.shape[1]), (0, 0))).reshape(RQ * 8, RQ * HB)
+    spread = jnp.repeat(places, 128, axis=-1)
+    onehot = (position[None, :, None] == spread[:, None, :]).astype(jnp.bfloat16)
+    allowed = jnp.einsum(
+        "otp,opn->otn",
+        jnp.broadcast_to(table[None], (8,) + table.shape),
+        onehot,
+        preferred_element_type=jnp.float32,
+    ) * (0.5 * DH ** (-0.5))
+    allowed = allowed.reshape(8, RQ, 8, 256)
+
+    rows = gates.shape[2]
+    vmem = pl.BlockSpec(memory_space=pltpu.VMEM)
+    bf16 = jnp.bfloat16
+    mixed = pl.pallas_call(
+        fused_kernel,
+        out_shape=jax.ShapeDtypeStruct((rows, H * DH), bf16),
+        in_specs=[pl.BlockSpec(memory_space=pltpu.SMEM)]
+        + [vmem] * 6
+        + [pl.BlockSpec(memory_space=pl.ANY)],
+        out_specs=vmem,
+        scratch_shapes=[
+            pltpu.VMEM((2, 8, 128, 256), bf16),
+            pltpu.VMEM((2, 8, 128, 256), bf16),
+            pltpu.VMEM((2, 8, 128, 256), bf16),
+            pltpu.VMEM((2, 8, 128, 256), bf16),
+            pltpu.VMEM((STAGES, 8, 2, 128, 256), bf16),
+            pltpu.VMEM((STAGES, 8, 2, 128, 256), bf16),
+            pltpu.VMEM((STAGES, 768, 128), bf16),
+            pltpu.VMEM((768, 128), jnp.float32),
+            pltpu.VMEM((STAGES, 8, 96, 128), bf16),
+            pltpu.VMEM((STAGES, 8, 96, 128), bf16),
+            pltpu.VMEM((8, 128, 1024), bf16),
+            pltpu.SemaphoreType.DMA((STAGES, 2)),
+            pltpu.SemaphoreType.DMA((STAGES, 8)),
+            pltpu.SemaphoreType.DMA((STAGES, 8)),
+            pltpu.SemaphoreType.DMA((4,)),
+            pltpu.SemaphoreType.DMA((4,)),
+            pltpu.SemaphoreType.DMA((STAGES, 8)),
+            pltpu.SemaphoreType.DMA((STAGES, 8)),
+            pltpu.SemaphoreType.DMA((8,)),
+            pltpu.SemaphoreType.DMA((8,)),
+        ],
+        compiler_params=pltpu.CompilerParams(
+            collective_id=0, has_side_effects=True, vmem_limit_bytes=40 * 1024 * 1024
+        ),
+        cost_estimate=pl.CostEstimate(
+            flops=4 * 4 * 768 * 2048 * 128, bytes_accessed=8 << 20, transcendentals=4 * 768 * 2048
+        ),
+    )(
+        send_rows,
+        allowed,
+        queries.reshape(queries.shape[2:]),
+        gates.reshape(rows, H * DH),
+        tokens.reshape(rows, H * DH),
+        w_out,
+        norm_gain.reshape(1, H * DH),
+        kv_cache,
+    )
+    return mixed.reshape(tokens.shape)
+
+
 def solution(mesh):
+    fused = mesh.shape["cuts"] == CUTS and mesh.shape["dev"] == DEVS
+    local = local_fused if fused else local_general
     return jax.shard_map(
         local,
         mesh=mesh,

time: 275 us -> 79 us (0.29)
  waiting for transfers between devices: 154 us -> 0 us
  Pallas kernels: 0 us -> 66.8 us
  local copies, waits for them, and re-layouts: 60.8 us -> 9.27 us
  matrix products: 21.1 us -> 0.31 us
  between operations: 13.5 us -> 0.04 us
  blocking collectives: 10.7 us -> 0 us
  starting transfers between devices: 10.3 us -> 0 us
    all_to_all x2 -> x0, waiting for transfers between devices: 154 us -> none  [the longest x1 107 us: local(): lax.all_to_all(outgoing, 'dev', split_axis=0, concat_axis=0, tiled=True)]
    pallas_call x0 -> x1, Pallas kernels: none -> 66.8 us  [local_fused(): pl.pallas_call(fused_kernel, out_shape=jax.ShapeDtypeStruct((rows, H * DH...]
    gather x10 -> x0, local copies, waits for them, and re-layouts: 26.7 us -> none  [the longest x4 11.5 us: attend(): blocks = flat_blocks[slot_rows]]
    dot_general x5 -> x1, matrix products: 21.1 us -> 0.31 us  [local_fused(): jnp.einsum('otp,opn->otn', jnp.broadcast_to(table[None], (8,) + table.sha...]
    scatter x1 -> x0, local copies, waits for them, and re-layouts: 10.9 us -> none  [local(): outgoing = outgoing.at[:, target].set(heads_first).reshape(dev_count, cap...]
    all_to_all x1 -> x0, blocking collectives: 10.7 us -> none  [local(): lax.all_to_all(attended.reshape(dev_count, rows_each, head_size), 'dev',...]
    all_to_all x2 -> x0, starting transfers between devices: 10.2 us -> none  [the longest x1 5.16 us: local(): lax.all_to_all(packed, 'cuts', split_axis=0, concat_axis=0, tiled=True)]
    slice x4 -> x0, local copies, waits for them, and re-layouts: 7.8 us -> none  [attend(): key_rows = blocks[:, :, :head_size].reshape(-1, head_size)]
  transfers between devices with their start and end apart: 3 -> 0, of which waited for: 2 -> 0; matrix products, arithmetic and copies ran while one was open for 17% -> 0% of each run, Pallas kernels for 0% -> 0%
where the time goes in v1:
time: 79 us; the launch traced here: 78.5 us
  Pallas kernels  66.8 us (85%)
  local copies, waits for them, and re-layouts  9.27 us (12%)
  other arithmetic  2.12 us (3%)
    pallas_call x1, Pallas kernels, local_fused(): pl.pallas_call(fused_kernel, out_shape=jax.ShapeDtypeStruct((rows, H * DH...  66.8 us
    unnamed x13, local copies, waits for them, and re-layouts  7.28 us

profile of v1, /device:TPU:0, one launch (start us, length us, event | category | flops | bytes accessed | tf_op | source)
XLA Modules:
  0.0 78.5 jit_solution(8547490622763229496)
XLA Ops:
  0.0 0.7 fusion.10
  0.7 0.1 iota_compare_fusion.3
  0.8 0.1 broadcast_in_dim.69
  0.9 0.1 broadcast_in_dim.70
  1.0 0.1 fusion.7
  1.0 0.7 constant_dynamic-slice_fusion
  1.7 0.1 eq.68
  1.8 0.2 fusion.4
  2.0 1.0 %select_reduce_fusion.1 = (s32[4]{0:T(128)S(1)}, s32[4]{0:T(128)S(1)}) fusion(s32[4,4,32]{2,1,0:T(4,128)} %param.20, s32[4,32]{1,0:T(4,128)S(1)} %add_multiply_fusion, s32[4,4,32]{2,1,0:T(4,128)} %param.19, s32[]{:T(128)S(6)} %add.53), kind=kLoop, calls=%fused_computation.10 | loop fusion | flops 3064 | bytes 4644 | tf_op jit(solution)/shard_map/reduce_min | solution.py:425
  3.0 0.1 copy.15
  3.1 0.1 copy.14
  3.2 0.1 add_select_fusion.rows_ref
  3.2 0.1 broadcast_bitcast_fusion
  3.3 0.7 fusion.3
  4.0 0.1 broadcast_in_dim.72
  4.1 0.3 fusion.mask_ref
  4.4 0.0 copy-start
  4.4 2.2 %copy-done = bf16[8,128,2048]{2,1,0:T(8,128)(2,1)S(1)} copy-done((bf16[8,128,2048]{2,1,0:T(8,128)(2,1)S(1)}, bf16[8,128,2048]{2,1,0:T(8,128)(2,1)}, u32[]{:S(2)}) %copy-start) | copy-done | bytes 4194328
  6.6 0.0 copy-start.1
  6.6 0.9 %copy-done.1 = bf16[128,1024]{1,0:T(8,128)(2,1)S(1)} copy-done((bf16[128,1024]{1,0:T(8,128)(2,1)S(1)}, bf16[128,1024]{1,0:T(8,128)(2,1)}, u32[]{:S(2)}) %copy-start.1) | copy-done | bytes 262168
  7.6 0.0 copy-start.2
  7.6 0.9 %copy-done.2 = bf16[1,1,768,128]{3,2,1,0:T(8,128)(2,1)S(1)} copy-done((bf16[1,1,768,128]{3,2,1,0:T(8,128)(2,1)S(1)}, bf16[1,1,768,128]{3,2,1,0:T(8,128)(2,1)}, u32[]{:S(2)}) %copy-start.2) | copy-done | bytes 196632
  8.5 0.0 copy-start.3
  8.5 0.9 %copy-done.3 = bf16[1,1,96,1024]{3,2,1,0:T(8,128)(2,1)S(1)} copy-done((bf16[1,1,96,1024]{3,2,1,0:T(8,128)(2,1)S(1)}, bf16[1,1,96,1024]{3,2,1,0:T(8,128)(2,1)}, u32[]{:S(2)}) %copy-start.3) | copy-done | bytes 196632
  9.4 0.0 copy-start.4
  9.4 0.9 %copy-done.4 = bf16[1,1,96,1024]{3,2,1,0:T(8,128)(2,1)S(1)} copy-done((bf16[1,1,96,1024]{3,2,1,0:T(8,128)(2,1)S(1)}, bf16[1,1,96,1024]{3,2,1,0:T(8,128)(2,1)}, u32[]{:S(2)}) %copy-start.4) | copy-done | bytes 196632
  10.4 0.0 copy-start.5
  10.4 0.7 copy-done.5
  11.1 66.8 %shard_map.109 = bf16[96,1024]{1,0:T(8,128)(2,1)S(1)} custom-call(s32[4,2]{1,0:T(4,128)S(1)} %add_select_fusion.rows_ref, f32[8,4,8,256]{3,2,1,0:T(8,128)S(1)} %fusion.mask_ref, bf16[768,128]{1,0:T(8,128)(2,1)S(1)} %bitcast.26, bf16[96,1024]{1,0:T(8,128)(2,1)S(1)} %bitcast.27, bf16[96,1024]{1,0:T(8,128)(2,1)S(1)} %bitcast.28, ...), custom_call_target="tpu_custom_call" | custom-call | flops 3221225472 | bytes 8388608 | tf_op jit(solution)/shard_map/pallas_call | solution.py:458
  77.8 0.7 copy.17
  (5 shorter events, 0.0 us)
Async XLA Ops:
  4.4 2.2 %copy-start = (bf16[8,128,2048]{2,1,0:T(8,128)(2,1)S(1)}, bf16[8,128,2048]{2,1,0:T(8,128)(2,1)}, u32[]{:S(2)}) copy-start(bf16[8,128,2048]{2,1,0:T(8,128)(2,1)} %kv_ref.1) | copy-start | bytes 12582916
  6.6 0.9 %copy-start.1 = (bf16[128,1024]{1,0:T(8,128)(2,1)S(1)}, bf16[128,1024]{1,0:T(8,128)(2,1)}, u32[]{:S(2)}) copy-start(bf16[128,1024]{1,0:T(8,128)(2,1)} %w_ref.1) | copy-start | bytes 786436
  7.6 0.9 %copy-start.2 = (bf16[1,1,768,128]{3,2,1,0:T(8,128)(2,1)S(1)}, bf16[1,1,768,128]{3,2,1,0:T(8,128)(2,1)}, u32[]{:S(2)}) copy-start(bf16[1,1,768,128]{3,2,1,0:T(8,128)(2,1)} %param.12) | copy-start | bytes 589828
  8.5 0.9 %copy-start.3 = (bf16[1,1,96,1024]{3,2,1,0:T(8,128)(2,1)S(1)}, bf16[1,1,96,1024]{3,2,1,0:T(8,128)(2,1)}, u32[]{:S(2)}) copy-start(bf16[1,1,96,1024]{3,2,1,0:T(8,128)(2,1)} %param.13) | copy-start | bytes 589828
  9.4 0.9 %copy-start.4 = (bf16[1,1,96,1024]{3,2,1,0:T(8,128)(2,1)S(1)}, bf16[1,1,96,1024]{3,2,1,0:T(8,128)(2,1)}, u32[]{:S(2)}) copy-start(bf16[1,1,96,1024]{3,2,1,0:T(8,128)(2,1)} %param.14) | copy-start | bytes 589828
  10.4 0.7 copy-start.5

commit v2 on v1

--- a/solution.py
+++ b/solution.py
@@ -152,15 +152,27 @@
 
 
 def fused_kernel(
-    rows_ref,
-    mask_ref,
-    q_ref,
+    hist_ref,
+    rank_ref,
+    owner_hbm,
+    slot_hbm,
+    seen_hbm,
+    q_hbm,
+    gates_hbm,
+    tokens_hbm,
+    w_hbm,
+    gain_hbm,
+    kv_hbm,
+    out_ref,
+    owner_ref,
+    slot_ref,
+    seen_ref,
     gates_ref,
     tokens_ref,
-    w_ref,
     gain_ref,
-    kv_ref,
-    out_ref,
+    rows_ref,
+    place_ref,
+    mask_ref,
     kv0,
     kv1,
     kv2,
@@ -181,6 +193,7 @@
     p_recv,
     w_send,
     w_recv,
+    table_sem,
 ):
     loaded = (kv0, kv1, kv2, kv3)
     cut = lax.axis_index("cuts")
@@ -198,12 +211,35 @@
         head = rem(z + s, 4) * 2 + core_at(oh)
         columns = pl.ds(pl.multiple_of(head * 256, 256), 256)
         return pltpu.make_async_copy(
-            kv_ref.at[:, :, columns], loaded[s].at[oh], load_sem.at[s, oh]
-        )
-
-    for s in range(STAGES):
+            kv_hbm.at[:, :, columns], loaded[s].at[oh], load_sem.at[s, oh]
+        )
+
+    fetch = [
+        pltpu.make_async_copy(source, target, table_sem.at[i])
+        for i, (source, target) in enumerate(
+            (
+                (owner_hbm, owner_ref),
+                (slot_hbm, slot_ref),
+                (seen_hbm, seen_ref),
+                (q_hbm, qbuf.at[0]),
+                (w_hbm, wbuf.at[z, 0]),
+                (gates_hbm, gates_ref),
+                (tokens_hbm, tokens_ref),
+                (gain_hbm, gain_ref),
+            )
+        )
+    ]
+    for i in (0, 1):
+        fetch[i].start()
+    for oh in range(2):
+        load(0, oh).start()
+    for i in (3, 2, 4):
+        fetch[i].start()
+    for s in range(1, STAGES):
         for oh in range(2):
             load(s, oh).start()
+    for i in (5, 6, 7):
+        fetch[i].start()
 
     barrier = pltpu.get_barrier_semaphore()
     for o in range(2, 8):
@@ -220,6 +256,16 @@
             device_id=(cut, rem(z + o // 2, 4) * 2 + core_at(o % 2)),
             device_id_type=MESH,
         )
+    position = lax.broadcasted_iota(jnp.int32, (RQ, HB), 0) * HB + lax.broadcasted_iota(
+        jnp.int32, (RQ, HB), 1
+    )
+    for i in (0, 1):
+        fetch[i].wait()
+    for oc in range(CUTS):
+        mine = owner_ref[cut_at(oc)] == cut * DEVS + dev
+        coded = position * DEVS + slot_ref[cut_at(oc)]
+        rows_ref[oc * 2] = rem(jnp.min(jnp.where(mine, coded, 1 << 20)), DEVS)
+        rows_ref[oc * 2 + 1] = rem(jnp.max(jnp.where(mine, coded, 0)), DEVS)
     pl.semaphore_wait(barrier, 13)
 
     def kv_copy(s, o):
@@ -234,7 +280,7 @@
 
     def q_copy(o):
         return pltpu.make_async_remote_copy(
-            src_ref=q_ref,
+            src_ref=qbuf.at[0],
             dst_ref=qbuf.at[4 - o],
             send_sem=q_send.at[4 - o],
             recv_sem=q_recv.at[4 - o],
@@ -253,21 +299,37 @@
             device_id_type=MESH,
         )
 
-    def w_copy(o):
-        if o % 2:
-            source = w_ref if o == 1 else wbuf.at[o - 1]
-            where = z * 2 + core_at(1)
-        else:
-            source = w_ref
-            where = rem(z + o // 2, 4) * 2 + core
+    def w_copy(zs, way):
+        where = (rem(z + 1, 4) * 2 + core, rem(z + 3, 4) * 2 + core, z * 2 + core_at(1))[way]
         return pltpu.make_async_remote_copy(
-            src_ref=source,
-            dst_ref=wbuf.at[o],
-            send_sem=w_send.at[o],
-            recv_sem=w_recv.at[o],
+            src_ref=wbuf.at[zs, 0],
+            dst_ref=wbuf.at[zs, way // 2],
+            send_sem=w_send.at[zs, way],
+            recv_sem=w_recv.at[zs, way // 2],
             device_id=(cut, where),
             device_id_type=MESH,
         )
+
+    def w_each(d, use):
+        for way, zs in ((0, z - d), (1, z + d)):
+
+            @pl.when((zs >= 0) & (zs < 4))
+            def _():
+                @pl.when((z < 3) if way == 0 else (z > 0))
+                def _():
+                    use(zs, way)
+
+                if d > 0 or way == 0:
+                    use(zs, 2)
+
+    def w_step(d):
+        for way, zs in ((0, z - d), (1, z + d)):
+
+            @pl.when((zs >= 0) & (zs < 4))
+            def _():
+                w_copy(zs, way).wait_recv()
+
+        w_each(d, lambda zs, way: w_copy(zs, way).start())
 
     def pack(s):
         for oh in range(2):
@@ -276,7 +338,7 @@
         def one(i, carry):
             oc = 3 - i
             for j in range(2):
-                slot = rows_ref[cut_at(oc), j]
+                slot = rows_ref[oc * 2 + j]
                 for oh in range(2):
                     pk[s, oc * 2 + oh, j] = loaded[s][oh, slot]
             for oh in range(2):
@@ -291,12 +353,30 @@
         rx[s, 0] = pk[s, 0]
 
     pack(0)
+    fetch[3].wait()
     for o in (3, 2, 1):
         q_copy(o).start()
     pack(1)
-    for o in (6, 4, 2, 1):
-        w_copy(o).start()
-    qbuf[0] = q_ref[...]
+    fetch[4].wait()
+    w_each(0, lambda zs, way: w_copy(zs, way).start())
+
+    owners = owner_ref[cut]
+    for o in range(8):
+        theirs = owners == cut_at(o // 2) * DEVS + z * 2 + core_at(o % 2)
+        lowest = jnp.min(jnp.where(theirs, position, 1 << 20))
+        highest = jnp.max(jnp.where(theirs, position, -1))
+        place_ref[:, o * 256 : o * 256 + 128] = jnp.full((1, 128), lowest, jnp.int32)
+        place_ref[:, o * 256 + 128 : o * 256 + 256] = jnp.full((1, 128), highest, jnp.int32)
+    fetch[2].wait()
+    for k in range(RQ):
+        request = rank_ref[cut, k]
+        seen = seen_ref[cut, request]
+        live = lax.broadcasted_iota(jnp.int32, seen.shape, 1) < hist_ref[cut, request]
+        seen = jnp.where(live, seen, 0).astype(jnp.float32).astype(jnp.bfloat16)
+        index = lax.broadcasted_iota(jnp.int32, (HB, 2048), 0) + request * HB
+        onehot = jnp.where(index == place_ref[...], 1.0, 0.0).astype(jnp.bfloat16)
+        allowed = jnp.dot(seen, onehot, preferred_element_type=jnp.float32)
+        mask_ref[k, 0:6, :] = allowed * (0.5 * DH ** (-0.5))
 
     def stage(s, carry):
         @pl.when(s > 0)
@@ -320,7 +400,8 @@
                     (((1,), (1,)), ((), ())),
                     preferred_element_type=jnp.float32,
                 )
-                half = scores.reshape(6, TILE, 256) * mask_ref[o, k][:6, None, :]
+                allowed = mask_ref[k, 0:6, pl.ds(pl.multiple_of(o * 256, 256), 256)]
+                half = scores.reshape(6, TILE, 256) * allowed[:, None, :]
                 weights = (half + half * jnp.tanh(half)).reshape(192, 256)
                 acc[rows, :] += jnp.dot(
                     weights.astype(jnp.bfloat16), values, preferred_element_type=jnp.float32
@@ -340,30 +421,32 @@
         @pl.when(s == 0)
         def _():
             pack(2)
+            w_step(1)
 
         @pl.when(s == 1)
         def _():
             pack(3)
+            w_step(2)
 
         @pl.when(s == 2)
         def _():
-            for o in (2, 4, 6):
-                w_copy(o).wait_recv()
-                w_copy(o + 1).start()
+            w_step(3)
 
         return carry
 
     lax.fori_loop(jnp.int32(0), jnp.int32(STAGES), stage, 0)
 
     gate_list, total_list = [], []
+    for i in (5, 6, 7):
+        fetch[i].wait()
     for pr in range(4):
         for oh in range(2):
             head = rem(z + pr, 4) * 2 + core_at(oh)
             columns = pl.ds(pl.multiple_of(head * 128, 128), 128)
             gate = gates_ref[:, columns].astype(jnp.float32)
             gate_list.append(gate / (1.0 + jnp.exp(-gate)) * gain_ref[:, columns])
-    for o in (1, 3, 5, 7):
-        w_copy(o).wait_recv()
+    for zs in range(4):
+        w_copy(zs, 2).wait_recv()
     for s in range(STAGES):
         for o in range(1, 8):
             p_copy(jnp.int32(s), jnp.int32(o)).wait_recv()
@@ -381,18 +464,17 @@
     scale = lax.rsqrt(variance + EPS)
     projected = tokens_ref[...].astype(jnp.float32)
     for pr in range(4):
-        ow = (4 - pr) % 4
+        zs = rem(z + pr, 4)
         for oh in range(2):
             r = pr * 2 + oh
             gated = (centred[r] * scale * gate_list[r]).astype(jnp.bfloat16)
-            weight = w_ref[...] if ow * 2 + oh == 0 else wbuf[ow * 2 + oh]
-            projected += jnp.dot(gated, weight, preferred_element_type=jnp.float32)
+            projected += jnp.dot(gated, wbuf[zs, oh], preferred_element_type=jnp.float32)
     out_ref[...] = projected.astype(out_ref.dtype)
 
     for o in (1, 2, 3):
         q_copy(o).wait_send()
-    for o in range(1, 8):
-        w_copy(o).wait_send()
+    for d in range(4):
+        w_each(d, lambda zs, way: w_copy(zs, way).wait_send())
 
     def drain(i, carry):
         s, o = div(i, 7), rem(i, 7) + 1
@@ -416,53 +498,25 @@
     slot_ids,
     block_mask,
 ):
-    cut = lax.axis_index("cuts")
-    dev = lax.axis_index("dev")
-    me = cut * DEVS + dev
-    position = jnp.arange(RQ * HB, dtype=jnp.int32)
-    coded = position * DEVS + slot_ids.reshape(CUTS, RQ * HB)
-    mine = owner_ids.reshape(CUTS, RQ * HB) == me
-    first = jnp.min(jnp.where(mine, coded, 1 << 20), axis=-1)
-    last = jnp.max(jnp.where(mine, coded, 0), axis=-1)
-    send_rows = jnp.stack([first, last], axis=-1) % DEVS
-
-    offset = jnp.arange(8, dtype=jnp.int32)
-    sources = (cut ^ (offset // 2)) * DEVS + (dev ^ (offset % 2))
-    owners = lax.dynamic_index_in_dim(owner_ids, cut, 0, keepdims=False).reshape(-1)
-    theirs = owners[None, :] == sources[:, None]
-    lowest = jnp.min(jnp.where(theirs, position, 1 << 20), axis=-1)
-    highest = jnp.max(jnp.where(theirs, position, -1), axis=-1)
-    places = jnp.stack([lowest, highest], axis=-1)
-    live = jnp.arange(HB, dtype=jnp.int32) < lax.dynamic_index_in_dim(
-        hist_blocks, cut, 0, keepdims=False
-    )[:, None]
-    visible = lax.dynamic_index_in_dim(block_mask, cut, 0, keepdims=False) * live[:, None, :]
-    ranks = lax.dynamic_index_in_dim(ranker_list, cut, 0, keepdims=False)
-    is_ranked = ranks[:, None] == jnp.arange(RQ, dtype=jnp.int32)
-    table = jnp.where(is_ranked[:, None, :, None], visible.transpose(1, 0, 2)[None], 0)
-    table = table.reshape(RQ, -1, RQ * HB).astype(jnp.bfloat16)
-    table = jnp.pad(table, ((0, 0), (0, 8 - table.shape[1]), (0, 0))).reshape(RQ * 8, RQ * HB)
-    spread = jnp.repeat(places, 128, axis=-1)
-    onehot = (position[None, :, None] == spread[:, None, :]).astype(jnp.bfloat16)
-    allowed = jnp.einsum(
-        "otp,opn->otn",
-        jnp.broadcast_to(table[None], (8,) + table.shape),
-        onehot,
-        preferred_element_type=jnp.float32,
-    ) * (0.5 * DH ** (-0.5))
-    allowed = allowed.reshape(8, RQ, 8, 256)
-
     rows = gates.shape[2]
     vmem = pl.BlockSpec(memory_space=pltpu.VMEM)
     bf16 = jnp.bfloat16
     mixed = pl.pallas_call(
         fused_kernel,
         out_shape=jax.ShapeDtypeStruct((rows, H * DH), bf16),
-        in_specs=[pl.BlockSpec(memory_space=pltpu.SMEM)]
-        + [vmem] * 6
-        + [pl.BlockSpec(memory_space=pl.ANY)],
+        in_specs=[pl.BlockSpec(memory_space=pltpu.SMEM)] * 2
+        + [pl.BlockSpec(memory_space=pl.ANY)] * 9,
         out_specs=vmem,
         scratch_shapes=[
+            pltpu.VMEM(owner_ids.shape, jnp.int32),
+            pltpu.VMEM(slot_ids.shape, jnp.int32),
+            pltpu.VMEM(block_mask.shape, jnp.int32),
+            pltpu.VMEM((rows, H * DH), bf16),
+            pltpu.VMEM((rows, H * DH), bf16),
+            pltpu.VMEM((1, H * DH), jnp.float32),
+            pltpu.SMEM((8,), jnp.int32),
+            pltpu.VMEM((1, 2048), jnp.int32),
+            pltpu.VMEM((RQ, 8, 2048), jnp.float32),
             pltpu.VMEM((2, 8, 128, 256), bf16),
             pltpu.VMEM((2, 8, 128, 256), bf16),
             pltpu.VMEM((2, 8, 128, 256), bf16),
@@ -473,7 +527,7 @@
             pltpu.VMEM((768, 128), jnp.float32),
             pltpu.VMEM((STAGES, 8, 96, 128), bf16),
             pltpu.VMEM((STAGES, 8, 96, 128), bf16),
-            pltpu.VMEM((8, 128, 1024), bf16),
+            pltpu.VMEM((4, 2, 128, 1024), bf16),
             pltpu.SemaphoreType.DMA((STAGES, 2)),
             pltpu.SemaphoreType.DMA((STAGES, 8)),
             pltpu.SemaphoreType.DMA((STAGES, 8)),
@@ -481,18 +535,22 @@
             pltpu.SemaphoreType.DMA((4,)),
             pltpu.SemaphoreType.DMA((STAGES, 8)),
             pltpu.SemaphoreType.DMA((STAGES, 8)),
-            pltpu.SemaphoreType.DMA((8,)),
+            pltpu.SemaphoreType.DMA((4, 3)),
+            pltpu.SemaphoreType.DMA((4, 2)),
             pltpu.SemaphoreType.DMA((8,)),
         ],
         compiler_params=pltpu.CompilerParams(
-            collective_id=0, has_side_effects=True, vmem_limit_bytes=40 * 1024 * 1024
+            collective_id=0, has_side_effects=True, vmem_limit_bytes=60 * 1024 * 1024
         ),
         cost_estimate=pl.CostEstimate(
             flops=4 * 4 * 768 * 2048 * 128, bytes_accessed=8 << 20, transcendentals=4 * 768 * 2048
         ),
     )(
-        send_rows,
-        allowed,
+        hist_blocks,
+        ranker_list,
+        owner_ids,
+        slot_ids,
+        block_mask,
         queries.reshape(queries.shape[2:]),
         gates.reshape(rows, H * DH),
         tokens.reshape(rows, H * DH),

time: 79 us -> 67.9 us (0.86)
  local copies, waits for them, and re-layouts: 9.27 us -> 3.05 us
  Pallas kernels: 66.8 us -> 64.5 us
  other arithmetic: 2.12 us -> 0 us
    unnamed x13 -> x2, local copies, waits for them, and re-layouts: 7.28 us -> 3.05 us
    pallas_call x1, Pallas kernels: 66.8 us -> 64.5 us  [local_fused(): pl.pallas_call(fused_kernel, out_shape=jax.ShapeDtypeStruct((rows, H * DH...]
    reduce_min x2 -> x0, other arithmetic: 1.14 us -> none  [the longest x1 0.95 us: local_fused(): first = jnp.min(jnp.where(mine, coded, 1 << 20), axis=-1)]
    eq x3 -> x0, local copies, waits for them, and re-layouts: 0.86 us -> none  [the longest x1 0.71 us: local_fused(): is_ranked = ranks[:, None] == jnp.arange(RQ, dtype=jnp.int32)]
where the time goes in v2:
time: 67.9 us; the launch traced here: 67.6 us
  Pallas kernels  64.5 us (95%)
  local copies, waits for them, and re-layouts  3.05 us (4%)
    pallas_call x1, Pallas kernels, local_fused(): pl.pallas_call(fused_kernel, out_shape=jax.ShapeDtypeStruct((rows, H * DH...  64.5 us
    unnamed x2, local copies, waits for them, and re-layouts  3.05 us

profile of v2, /device:TPU:0, one launch (start us, length us, event | category | flops | bytes accessed | tf_op | source)
XLA Modules:
  0.0 67.6 jit_solution(18180095265674172993)
XLA Ops:
  0.0 1.4 %copy.12.seen_hbm = s32[4,4,6,32]{3,2,1,0:T(8,128)} copy(s32[4,4,6,32]{3,1,2,0:T(4,128)} %param.21) | data formatting | bytes 24576 | tf_op args[10]
  1.4 64.5 %shard_map.109 = bf16[96,1024]{1,0:T(8,128)(2,1)} custom-call(s32[4,4]{1,0:T(4,128)} %hist_ref.1, s32[4,4]{1,0:T(4,128)} %rank_ref.1, s32[4,4,32]{2,1,0:T(4,128)} %owner_hbm.1, s32[4,4,32]{2,1,0:T(4,128)} %slot_hbm.1, s32[4,4,6,32]{3,2,1,0:T(8,128)} %copy.12.seen_hbm, bf16[768,128]{1,0:T(8,128)(2,1)} %bitcast.6, bf16[96,1024]{1,0:T(8,128)(2,1)} %bitcast.7, ...), custom_call_target="tpu_custom_call" | custom-call | flops 3221225472 | bytes 8388608 | tf_op jit(solution)/shard_map/pallas_call | solution.py:504
  66.0 1.6 %copy.14 = bf16[1,1,96,1024]{3,2,1,0:T(8,128)(2,1)} copy(bf16[1,1,96,1024]{3,2,1,0:T(8,128)(2,1)} %bitcast.5) | data formatting | bytes 393216

commit v3 on v2

--- a/solution.py
+++ b/solution.py
@@ -171,6 +171,7 @@
     tokens_ref,
     gain_ref,
     rows_ref,
+    slot_of_ref,
     place_ref,
     mask_ref,
     kv0,
@@ -180,6 +181,7 @@
     pk,
     rx,
     qbuf,
+    qnow,
     acc,
     ab,
     parts,
@@ -365,18 +367,25 @@
         theirs = owners == cut_at(o // 2) * DEVS + z * 2 + core_at(o % 2)
         lowest = jnp.min(jnp.where(theirs, position, 1 << 20))
         highest = jnp.max(jnp.where(theirs, position, -1))
-        place_ref[:, o * 256 : o * 256 + 128] = jnp.full((1, 128), lowest, jnp.int32)
-        place_ref[:, o * 256 + 128 : o * 256 + 256] = jnp.full((1, 128), highest, jnp.int32)
+        for j, place in enumerate((lowest, highest)):
+            n = o * 2 + j
+            place_ref[:, n * 128 : n * 128 + 128] = jnp.full((1, 128), place, jnp.int32)
+            ranked_at = jnp.int32(0)
+            for k in range(1, RQ):
+                ranked_at += jnp.where(rank_ref[cut, k] == div(place, HB), k, 0)
+            slot_of_ref[n] = jnp.minimum(ranked_at, RQ - 1)
     fetch[2].wait()
-    for k in range(RQ):
-        request = rank_ref[cut, k]
-        seen = seen_ref[cut, request]
-        live = lax.broadcasted_iota(jnp.int32, seen.shape, 1) < hist_ref[cut, request]
+    allowed = jnp.zeros((6, 2048), jnp.float32)
+    for r in range(RQ):
+        seen = seen_ref[cut, :, r, :]
+        live = lax.broadcasted_iota(jnp.int32, seen.shape, 1) < hist_ref[cut, r]
         seen = jnp.where(live, seen, 0).astype(jnp.float32).astype(jnp.bfloat16)
-        index = lax.broadcasted_iota(jnp.int32, (HB, 2048), 0) + request * HB
+        index = lax.broadcasted_iota(jnp.int32, (HB, 2048), 0) + r * HB
         onehot = jnp.where(index == place_ref[...], 1.0, 0.0).astype(jnp.bfloat16)
-        allowed = jnp.dot(seen, onehot, preferred_element_type=jnp.float32)
-        mask_ref[k, 0:6, :] = allowed * (0.5 * DH ** (-0.5))
+        allowed += jnp.dot(seen, onehot, preferred_element_type=jnp.float32)
+    allowed = allowed * (0.5 * DH ** (-0.5))
+    for n in range(16):
+        mask_ref[n, 0:6, :] = allowed[:, n * 128 : n * 128 + 128]
 
     def stage(s, carry):
         @pl.when(s > 0)
@@ -384,28 +393,35 @@
             q_copy(4 - s).wait_recv()
 
         acc[...] = jnp.zeros_like(acc)
+        qnow[...] = qbuf[s].reshape(RQ, 192, 128)
 
         def block(o, inner):
             @pl.when(o > 0)
             def _():
                 kv_copy(s, o).wait_recv()
 
-            keys = rx[s, o, :, :, 0:128].reshape(256, 128)
-            values = rx[s, o, :, :, 128:256].reshape(256, 128)
-            for k in range(RQ):
-                rows = pl.ds(k * 192, 192)
+            products, factors = [], []
+            for j in range(2):
+                n = o * 2 + j
+                where = slot_of_ref[n]
                 scores = lax.dot_general(
-                    qbuf[s, rows, :],
-                    keys,
+                    qnow[where],
+                    rx[s, o, j, :, 0:128],
                     (((1,), (1,)), ((), ())),
                     preferred_element_type=jnp.float32,
                 )
-                allowed = mask_ref[k, 0:6, pl.ds(pl.multiple_of(o * 256, 256), 256)]
-                half = scores.reshape(6, TILE, 256) * allowed[:, None, :]
-                weights = (half + half * jnp.tanh(half)).reshape(192, 256)
-                acc[rows, :] += jnp.dot(
-                    weights.astype(jnp.bfloat16), values, preferred_element_type=jnp.float32
+                half = scores.reshape(6, TILE, 128) * mask_ref[n, 0:6, :][:, None, :]
+                weights = (half + half * jnp.tanh(half)).reshape(192, 128)
+                products.append(
+                    jnp.dot(
+                        weights.astype(jnp.bfloat16),
+                        rx[s, o, j, :, 128:256],
+                        preferred_element_type=jnp.float32,
+                    )
                 )
+                factors.append([jnp.where(where == k, 1.0, 0.0) for k in range(RQ)])
+            for k in range(RQ):
+                acc[k] += products[0] * factors[0][k] + products[1] * factors[1][k]
             return inner
 
         lax.fori_loop(jnp.int32(0), jnp.int32(8), block, 0)
@@ -498,6 +514,7 @@
     slot_ids,
     block_mask,
 ):
+    seen = block_mask.transpose(0, 2, 1, 3)
     rows = gates.shape[2]
     vmem = pl.BlockSpec(memory_space=pltpu.VMEM)
     bf16 = jnp.bfloat16
@@ -510,13 +527,14 @@
         scratch_shapes=[
             pltpu.VMEM(owner_ids.shape, jnp.int32),
             pltpu.VMEM(slot_ids.shape, jnp.int32),
-            pltpu.VMEM(block_mask.shape, jnp.int32),
+            pltpu.VMEM(seen.shape, jnp.int32),
             pltpu.VMEM((rows, H * DH), bf16),
             pltpu.VMEM((rows, H * DH), bf16),
             pltpu.VMEM((1, H * DH), jnp.float32),
             pltpu.SMEM((8,), jnp.int32),
+            pltpu.SMEM((16,), jnp.int32),
             pltpu.VMEM((1, 2048), jnp.int32),
-            pltpu.VMEM((RQ, 8, 2048), jnp.float32),
+            pltpu.VMEM((16, 8, 128), jnp.float32),
             pltpu.VMEM((2, 8, 128, 256), bf16),
             pltpu.VMEM((2, 8, 128, 256), bf16),
             pltpu.VMEM((2, 8, 128, 256), bf16),
@@ -524,7 +542,8 @@
             pltpu.VMEM((STAGES, 8, 2, 128, 256), bf16),
             pltpu.VMEM((STAGES, 8, 2, 128, 256), bf16),
             pltpu.VMEM((STAGES, 768, 128), bf16),
-            pltpu.VMEM((768, 128), jnp.float32),
+            pltpu.VMEM((RQ, 192, 128), bf16),
+            pltpu.VMEM((RQ, 192, 128), jnp.float32),
             pltpu.VMEM((STAGES, 8, 96, 128), bf16),
             pltpu.VMEM((STAGES, 8, 96, 128), bf16),
             pltpu.VMEM((4, 2, 128, 1024), bf16),
@@ -550,7 +569,7 @@
         ranker_list,
         owner_ids,
         slot_ids,
-        block_mask,
+        seen,
         queries.reshape(queries.shape[2:]),
         gates.reshape(rows, H * DH),
         tokens.reshape(rows, H * DH),

time: 67.9 us -> 65.7 us (0.968)
  local copies, waits for them, and re-layouts: 3.05 us -> 1.62 us
  Pallas kernels: 64.5 us -> 63.8 us
    unnamed x2 -> x1, local copies, waits for them, and re-layouts: 3.05 us -> 1.62 us
    pallas_call x1, Pallas kernels: 64.5 us -> 63.8 us  [local_fused(): pl.pallas_call(fused_kernel, out_shape=jax.ShapeDtypeStruct((rows, H * DH...]
where the time goes in v3:
time: 65.7 us; the launch traced here: 65.5 us
  Pallas kernels  63.8 us (97%)
  local copies, waits for them, and re-layouts  1.62 us (2%)
    pallas_call x1, Pallas kernels, local_fused(): pl.pallas_call(fused_kernel, out_shape=jax.ShapeDtypeStruct((rows, H * DH...  63.8 us
    unnamed x1, local copies, waits for them, and re-layouts  1.62 us

profile of v3, /device:TPU:0, one launch (start us, length us, event | category | flops | bytes accessed | tf_op | source)
XLA Modules:
  0.0 65.5 jit_solution(10163756825667660381)
XLA Ops:
  0.0 63.8 %shard_map.109 = bf16[96,1024]{1,0:T(8,128)(2,1)} custom-call(s32[4,4]{1,0:T(4,128)} %hist_ref.1, s32[4,4]{1,0:T(4,128)} %rank_ref.1, s32[4,4,32]{2,1,0:T(4,128)} %owner_hbm.1, s32[4,4,32]{2,1,0:T(4,128)} %slot_hbm.1, s32[4,6,4,32]{3,2,1,0:T(4,128)} %bitcast.10, bf16[768,128]{1,0:T(8,128)(2,1)} %bitcast.7, bf16[96,1024]{1,0:T(8,128)(2,1)} %bitcast.8, ...), custom_call_target="tpu_custom_call" | custom-call | flops 3221225472 | bytes 8388608 | tf_op jit(solution)/shard_map/pallas_call | solution.py:521
  63.8 1.6 %copy.13 = bf16[1,1,96,1024]{3,2,1,0:T(8,128)(2,1)} copy(bf16[1,1,96,1024]{3,2,1,0:T(8,128)(2,1)} %bitcast.6) | data formatting | bytes 393216

commit v4 on v3

--- a/solution.py
+++ b/solution.py
@@ -333,7 +333,7 @@
 
         w_each(d, lambda zs, way: w_copy(zs, way).start())
 
-    def pack(s):
+    def pack(s, now):
         for oh in range(2):
             load(s, oh).wait()
 
@@ -344,23 +344,26 @@
                 for oh in range(2):
                     pk[s, oc * 2 + oh, j] = loaded[s][oh, slot]
             for oh in range(2):
-
-                @pl.when(oc * 2 + oh > 0)
-                def _():
-                    kv_copy(s, oc * 2 + oh).start()
+                if now:
+
+                    @pl.when(oc * 2 + oh > 0)
+                    def _():
+                        kv_copy(s, oc * 2 + oh).start()
 
             return carry
 
         lax.fori_loop(jnp.int32(0), jnp.int32(4), one, 0)
         rx[s, 0] = pk[s, 0]
 
-    pack(0)
+    pack(0, True)
     fetch[3].wait()
     for o in (3, 2, 1):
         q_copy(o).start()
-    pack(1)
+    pack(1, True)
     fetch[4].wait()
     w_each(0, lambda zs, way: w_copy(zs, way).start())
+    pack(2, True)
+    pack(3, False)
 
     owners = owner_ref[cut]
     for o in range(8):
@@ -400,6 +403,10 @@
             def _():
                 kv_copy(s, o).wait_recv()
 
+                @pl.when(s == 0)
+                def _():
+                    kv_copy(3, o).start()
+
             products, factors = [], []
             for j in range(2):
                 n = o * 2 + j
@@ -436,12 +443,10 @@
 
         @pl.when(s == 0)
         def _():
-            pack(2)
             w_step(1)
 
         @pl.when(s == 1)
         def _():
-            pack(3)
             w_step(2)
 
         @pl.when(s == 2)

time: 65.7 us -> 64.9 us (0.988)
  Pallas kernels: 63.8 us -> 62.8 us
    pallas_call x1, Pallas kernels: 63.8 us -> 62.8 us  [local_fused(): pl.pallas_call(fused_kernel, out_shape=jax.ShapeDtypeStruct((rows, H * DH...]
where the time goes in v4:
time: 64.9 us; the launch traced here: 64.4 us
  Pallas kernels  62.8 us (97%)
  local copies, waits for them, and re-layouts  1.62 us (2%)
    pallas_call x1, Pallas kernels, local_fused(): pl.pallas_call(fused_kernel, out_shape=jax.ShapeDtypeStruct((rows, H * DH...  62.8 us
    unnamed x1, local copies, waits for them, and re-layouts  1.62 us

profile of v4, /device:TPU:0, one launch (start us, length us, event | category | flops | bytes accessed | tf_op | source)
XLA Modules:
  0.0 64.4 jit_solution(4658403923426307118)
XLA Ops:
  0.0 62.8 %shard_map.109 = bf16[96,1024]{1,0:T(8,128)(2,1)} custom-call(s32[4,4]{1,0:T(4,128)} %hist_ref.1, s32[4,4]{1,0:T(4,128)} %rank_ref.1, s32[4,4,32]{2,1,0:T(4,128)} %owner_hbm.1, s32[4,4,32]{2,1,0:T(4,128)} %slot_hbm.1, s32[4,6,4,32]{3,2,1,0:T(4,128)} %bitcast.10, bf16[768,128]{1,0:T(8,128)(2,1)} %bitcast.7, bf16[96,1024]{1,0:T(8,128)(2,1)} %bitcast.8, ...), custom_call_target="tpu_custom_call" | custom-call | flops 3221225472 | bytes 8388608 | tf_op jit(solution)/shard_map/pallas_call | solution.py:526
  62.8 1.6 %copy.13 = bf16[1,1,96,1024]{3,2,1,0:T(8,128)(2,1)} copy(bf16[1,1,96,1024]{3,2,1,0:T(8,128)(2,1)} %bitcast.6) | data formatting | bytes 393216

commit v5 on v4

--- a/solution.py
+++ b/solution.py
@@ -223,7 +223,7 @@
                 (owner_hbm, owner_ref),
                 (slot_hbm, slot_ref),
                 (seen_hbm, seen_ref),
-                (q_hbm, qbuf.at[0]),
+                (q_hbm, qbuf.at[z]),
                 (w_hbm, wbuf.at[z, 0]),
                 (gates_hbm, gates_ref),
                 (tokens_hbm, tokens_ref),
@@ -280,13 +280,13 @@
             device_id_type=MESH,
         )
 
-    def q_copy(o):
+    def q_copy(zs, way):
         return pltpu.make_async_remote_copy(
-            src_ref=qbuf.at[0],
-            dst_ref=qbuf.at[4 - o],
-            send_sem=q_send.at[4 - o],
-            recv_sem=q_recv.at[4 - o],
-            device_id=(cut, rem(z + o, 4) * 2 + core),
+            src_ref=qbuf.at[zs],
+            dst_ref=qbuf.at[zs],
+            send_sem=q_send.at[zs, way],
+            recv_sem=q_recv.at[zs],
+            device_id=(cut, rem(z + 1 + 2 * way, 4) * 2 + core),
             device_id_type=MESH,
         )
 
@@ -312,7 +312,7 @@
             device_id_type=MESH,
         )
 
-    def w_each(d, use):
+    def w_each(d, use, partner=True):
         for way, zs in ((0, z - d), (1, z + d)):
 
             @pl.when((zs >= 0) & (zs < 4))
@@ -321,8 +321,17 @@
                 def _():
                     use(zs, way)
 
-                if d > 0 or way == 0:
+                if partner and (d > 0 or way == 0):
                     use(zs, 2)
+
+    def q_step(d):
+        for way, zs in ((0, z - d), (1, z + d)):
+
+            @pl.when((zs >= 0) & (zs < 4))
+            def _():
+                q_copy(zs, way).wait_recv()
+
+        w_each(d, lambda zs, way: q_copy(zs, way).start(), False)
 
     def w_step(d):
         for way, zs in ((0, z - d), (1, z + d)):
@@ -357,12 +366,9 @@
 
     pack(0, True)
     fetch[3].wait()
-    for o in (3, 2, 1):
-        q_copy(o).start()
+    w_each(0, lambda zs, way: q_copy(zs, way).start(), False)
     pack(1, True)
-    fetch[4].wait()
-    w_each(0, lambda zs, way: w_copy(zs, way).start())
-    pack(2, True)
+    pack(2, False)
     pack(3, False)
 
     owners = owner_ref[cut]
@@ -390,22 +396,24 @@
     for n in range(16):
         mask_ref[n, 0:6, :] = allowed[:, n * 128 : n * 128 + 128]
 
+    for d in (1, 2):
+        q_step(d)
+    fetch[4].wait()
+    w_each(0, lambda zs, way: w_copy(zs, way).start())
+    q_step(3)
+
     def stage(s, carry):
-        @pl.when(s > 0)
-        def _():
-            q_copy(4 - s).wait_recv()
-
         acc[...] = jnp.zeros_like(acc)
-        qnow[...] = qbuf[s].reshape(RQ, 192, 128)
+        qnow[...] = qbuf[rem(z + s, 4)].reshape(RQ, 192, 128)
 
         def block(o, inner):
             @pl.when(o > 0)
             def _():
                 kv_copy(s, o).wait_recv()
 
-                @pl.when(s == 0)
+                @pl.when(s < 2)
                 def _():
-                    kv_copy(3, o).start()
+                    kv_copy(s + 2, o).start()
 
             products, factors = [], []
             for j in range(2):
@@ -468,15 +476,35 @@
             gate_list.append(gate / (1.0 + jnp.exp(-gate)) * gain_ref[:, columns])
     for zs in range(4):
         w_copy(zs, 2).wait_recv()
-    for s in range(STAGES):
-        for o in range(1, 8):
-            p_copy(jnp.int32(s), jnp.int32(o)).wait_recv()
+    for d in range(4):
+        w_each(d, lambda zs, way: q_copy(zs, way).wait_send(), False)
+        w_each(d, lambda zs, way: w_copy(zs, way).wait_send())
+
+    def drain(i, carry):
+        s, o = div(i, 7), rem(i, 7) + 1
+        kv_copy(s, o).wait_send()
+
+        @pl.when(s < 3)
+        def _():
+            p_copy(s, o).wait_send()
+            p_copy(s, o).wait_recv()
+
+        return carry
+
+    lax.fori_loop(jnp.int32(0), jnp.int32(28), drain, 0)
     for pr in range(4):
         for oh in range(2):
-            total = parts[pr, oh].astype(jnp.float32)
-            for ok in range(1, 4):
+            early = [ok for ok in range(4) if (pr + ok) % 4 < 3]
+            total = parts[(pr + early[0]) % 4, early[0] * 2 + oh].astype(jnp.float32)
+            for ok in early[1:]:
                 total += parts[(pr + ok) % 4, ok * 2 + oh].astype(jnp.float32)
             total_list.append(total)
+    for o in range(1, 8):
+        p_copy(jnp.int32(3), jnp.int32(o)).wait_recv()
+    for pr in range(4):
+        for oh in range(2):
+            late = parts[3, (3 - pr) * 2 + oh].astype(jnp.float32)
+            total_list[pr * 2 + oh] += late
     features = float(H * DH)
     mean = jnp.sum(sum(total_list), axis=-1, keepdims=True) / features
     centred = [total - mean for total in total_list]
@@ -486,24 +514,15 @@
     projected = tokens_ref[...].astype(jnp.float32)
     for pr in range(4):
         zs = rem(z + pr, 4)
-        for oh in range(2):
-            r = pr * 2 + oh
-            gated = (centred[r] * scale * gate_list[r]).astype(jnp.bfloat16)
-            projected += jnp.dot(gated, wbuf[zs, oh], preferred_element_type=jnp.float32)
+        gated = jnp.concatenate(
+            [centred[r] * scale * gate_list[r] for r in (pr * 2, pr * 2 + 1)], axis=-1
+        ).astype(jnp.bfloat16)
+        weight = wbuf[zs].reshape(2 * DH, H * DH)
+        projected += jnp.dot(gated, weight, preferred_element_type=jnp.float32)
     out_ref[...] = projected.astype(out_ref.dtype)
 
-    for o in (1, 2, 3):
-        q_copy(o).wait_send()
-    for d in range(4):
-        w_each(d, lambda zs, way: w_copy(zs, way).wait_send())
-
-    def drain(i, carry):
-        s, o = div(i, 7), rem(i, 7) + 1
-        kv_copy(s, o).wait_send()
-        p_copy(s, o).wait_send()
-        return carry
-
-    lax.fori_loop(jnp.int32(0), jnp.int32(28), drain, 0)
+    for o in range(1, 8):
+        p_copy(jnp.int32(3), jnp.int32(o)).wait_send()
 
 
 def local_fused(
@@ -555,7 +574,7 @@
             pltpu.SemaphoreType.DMA((STAGES, 2)),
             pltpu.SemaphoreType.DMA((STAGES, 8)),
             pltpu.SemaphoreType.DMA((STAGES, 8)),
-            pltpu.SemaphoreType.DMA((4,)),
+            pltpu.SemaphoreType.DMA((4, 2)),
             pltpu.SemaphoreType.DMA((4,)),
             pltpu.SemaphoreType.DMA((STAGES, 8)),
             pltpu.SemaphoreType.DMA((STAGES, 8)),

time: 64.9 us -> 64 us (0.986)
  Pallas kernels: 62.8 us -> 62.1 us
    pallas_call x1, Pallas kernels: 62.8 us -> 62.1 us  [local_fused(): pl.pallas_call(fused_kernel, out_shape=jax.ShapeDtypeStruct((rows, H * DH...]
where the time goes in v5:
time: 64 us; the launch traced here: 63.7 us
  Pallas kernels  62.1 us (97%)
  local copies, waits for them, and re-layouts  1.62 us (3%)
    pallas_call x1, Pallas kernels, local_fused(): pl.pallas_call(fused_kernel, out_shape=jax.ShapeDtypeStruct((rows, H * DH...  62.1 us
    unnamed x1, local copies, waits for them, and re-layouts  1.62 us

profile of v5, /device:TPU:0, one launch (start us, length us, event | category | flops | bytes accessed | tf_op | source)
XLA Modules:
  0.0 63.7 jit_solution(12006075018196908225)
XLA Ops:
  0.0 62.1 %shard_map.109 = bf16[96,1024]{1,0:T(8,128)(2,1)} custom-call(s32[4,4]{1,0:T(4,128)} %hist_ref.1, s32[4,4]{1,0:T(4,128)} %rank_ref.1, s32[4,4,32]{2,1,0:T(4,128)} %owner_hbm.1, s32[4,4,32]{2,1,0:T(4,128)} %slot_hbm.1, s32[4,6,4,32]{3,2,1,0:T(4,128)} %bitcast.10, bf16[768,128]{1,0:T(8,128)(2,1)} %bitcast.7, bf16[96,1024]{1,0:T(8,128)(2,1)} %bitcast.8, ...), custom_call_target="tpu_custom_call" | custom-call | flops 3221225472 | bytes 8388608 | tf_op jit(solution)/shard_map/pallas_call | solution.py:545
  62.1 1.6 %copy.13 = bf16[1,1,96,1024]{3,2,1,0:T(8,128)(2,1)} copy(bf16[1,1,96,1024]{3,2,1,0:T(8,128)(2,1)} %bitcast.6) | data formatting | bytes 393216

commit v6 on v5

--- a/solution.py
+++ b/solution.py
@@ -364,9 +364,11 @@
         lax.fori_loop(jnp.int32(0), jnp.int32(4), one, 0)
         rx[s, 0] = pk[s, 0]
 
-    pack(0, True)
     fetch[3].wait()
     w_each(0, lambda zs, way: q_copy(zs, way).start(), False)
+    pack(0, True)
+    fetch[4].wait()
+    w_each(0, lambda zs, way: w_copy(zs, way).start())
     pack(1, True)
     pack(2, False)
     pack(3, False)
@@ -398,8 +400,7 @@
 
     for d in (1, 2):
         q_step(d)
-    fetch[4].wait()
-    w_each(0, lambda zs, way: w_copy(zs, way).start())
+    w_step(1)
     q_step(3)
 
     def stage(s, carry):
@@ -451,13 +452,9 @@
 
         @pl.when(s == 0)
         def _():
-            w_step(1)
+            w_step(2)
 
         @pl.when(s == 1)
-        def _():
-            w_step(2)
-
-        @pl.when(s == 2)
         def _():
             w_step(3)
 

time: 64 us -> 64 us (level)
  no operation moved by 1% of the time
where the time goes in v6:
time: 64 us; the launch traced here: 63.7 us
  Pallas kernels  62.1 us (97%)
  local copies, waits for them, and re-layouts  1.62 us (3%)
    pallas_call x1, Pallas kernels, local_fused(): pl.pallas_call(fused_kernel, out_shape=jax.ShapeDtypeStruct((rows, H * DH...  62.1 us
    unnamed x1, local copies, waits for them, and re-layouts  1.62 us

profile of v6, /device:TPU:0, one launch (start us, length us, event | category | flops | bytes accessed | tf_op | source)
XLA Modules:
  0.0 63.7 jit_solution(3059666069741308551)
XLA Ops:
  0.0 62.1 %shard_map.109 = bf16[96,1024]{1,0:T(8,128)(2,1)} custom-call(s32[4,4]{1,0:T(4,128)} %hist_ref.1, s32[4,4]{1,0:T(4,128)} %rank_ref.1, s32[4,4,32]{2,1,0:T(4,128)} %owner_hbm.1, s32[4,4,32]{2,1,0:T(4,128)} %slot_hbm.1, s32[4,6,4,32]{3,2,1,0:T(4,128)} %bitcast.10, bf16[768,128]{1,0:T(8,128)(2,1)} %bitcast.7, bf16[96,1024]{1,0:T(8,128)(2,1)} %bitcast.8, ...), custom_call_target="tpu_custom_call" | custom-call | flops 3221225472 | bytes 8388608 | tf_op jit(solution)/shard_map/pallas_call | solution.py:542
  62.1 1.6 %copy.13 = bf16[1,1,96,1024]{3,2,1,0:T(8,128)(2,1)} copy(bf16[1,1,96,1024]{3,2,1,0:T(8,128)(2,1)} %bitcast.6) | data formatting | bytes 393216
